TPU v7x, 32 devices: a whole 2x2x4 slice. The times are simulated.
32 devices in a mesh: head: 4 (over x, core), seq: 8 (over z, y).
Axes of the slice: x: 2, y: 2, z: 4, core: 2. Of those that a mesh axis runs over, the one named last changes fastest.
Arguments:
- queries: bfloat16 [4, 1024, 3584], P('head', 'seq'), may hold values from -16 to 16
- trunk_keys: bfloat16 [1024, 512], P('seq', 'head'), may hold values from -16 to 16
- trunk_values: bfloat16 [1024, 512], P('seq', 'head'), may hold values from -6 to 6
- out_grad: bfloat16 [4, 1024, 3584], P('head', 'seq'), may hold values from -6 to 6
- segment_ids: int32 [1024], P('seq'), may hold values from 0 to 3, never falling along the last dimension, each value on 1 to 512 neighbouring positions
Outputs:
- attended: bfloat16 [4, 1024, 3584], P('head', 'seq')
- query_grad: bfloat16 [4, 1024, 3584], P('head', 'seq')
- key_grad: float32 [1024, 512], P('seq', 'head')
- value_grad: float32 [1024, 512], P('seq', 'head')
Inputs may be any that keep to these rules, and one draw needn't show every extreme that they name: `segment_ids`: documents are runs of consecutive tokens; one has exactly 512 tokens and none has more.
All inputs are finite; a program needn't handle non-finite values.
Results may differ from a plain program's by a relative error of at most 0.012.
Values may be sent and summed in bfloat16 or wider, within the bound.
A program may use at most 64 MiB of HBM per device.

v0:
```python
import math

import jax
import jax.numpy as jnp
from jax import lax
from jax.sharding import PartitionSpec as P

DH = 128
QH = 28
SPAN = 4


def as_sent(x):

    def short(part):
        return part.astype(jnp.bfloat16) if part.dtype == jnp.float32 else part

    return jax.tree.map(short, x)


def from_behind(value, axis, steps):
    count = lax.axis_size(axis)
    leading, last = (max(0, -steps), min(count, count - steps))
    return lax.ppermute(value, axis, [(source, source + steps) for source in range(leading, last)])


def shards(queries, trunk_keys, trunk_values, out_grad, segment_ids):
    keys_all, values_all = (
        lax.all_gather(trunk_keys, "head", axis=1, tiled=True),
        lax.all_gather(trunk_values, "head", axis=1, tiled=True),
    )
    tok_rows = keys_all.shape[0]
    kv_heads = keys_all.shape[1] // DH
    q_group = QH // kv_heads
    scaling = 1.0 / math.sqrt(DH)
    query_rows = queries[0].reshape(tok_rows, kv_heads, q_group, DH)
    grad_rows = out_grad[0].reshape(tok_rows, kv_heads, q_group, DH)
    cycle_size = lax.axis_size("seq")
    my_index = lax.axis_index("seq")
    offsets = jnp.arange(tok_rows, dtype=jnp.int32)
    query_pos = my_index * tok_rows + offsets
    home_block = (keys_all, values_all, segment_ids)
    blocks = [home_block]
    for hop_count in range(1, SPAN + 1):
        blocks.append(from_behind(as_sent(blocks[-1]), "seq", 1))
    masks = []
    for hop_count in range(SPAN + 1):
        anchor = (my_index - hop_count) % cycle_size
        key_pos = anchor * tok_rows + offsets
        masks.append(
            (blocks[hop_count][2][None, :] == segment_ids[:, None])
            & (key_pos[None, :] <= query_pos[:, None])
        )

    def scores_of(block, allowed):
        key_blk = block[0].reshape(tok_rows, kv_heads, DH)
        raw = (
            jnp.einsum("igrd,jgd->grij", query_rows, key_blk, preferred_element_type=jnp.float32)
            * scaling
        )
        return jnp.where(allowed[None, None], raw, -1e30)

    row_top = jnp.full((kv_heads, q_group, tok_rows), -1e30, jnp.float32)
    row_total = jnp.zeros((kv_heads, q_group, tok_rows), jnp.float32)
    kept_scores = []
    for hop_count in range(SPAN + 1):

        def update_stats(
            block=blocks[hop_count], allowed=masks[hop_count], old_top=row_top, old_total=row_total
        ):
            scores = scores_of(block, allowed)
            new_top = jnp.maximum(old_top, jnp.max(scores, axis=-1))
            new_total = old_total * jnp.exp(old_top - new_top) + jnp.sum(
                jnp.exp(scores - new_top[..., None]), axis=-1
            )
            return (new_top, new_total, scores)

        row_top, row_total, scores_now = update_stats()
        kept_scores.append(scores_now)

    def probs_of(hop_count):
        return jnp.exp(kept_scores[hop_count] - row_top[..., None]) / row_total[..., None]

    out_acc = jnp.zeros((tok_rows, kv_heads, q_group, DH), jnp.float32)
    for hop_count in range(SPAN + 1):

        def add_values(hop_count=hop_count, block=blocks[hop_count], old_acc=out_acc):
            probs_b = probs_of(hop_count).astype(jnp.bfloat16)
            value_blk = block[1].reshape(tok_rows, kv_heads, DH)
            return old_acc + jnp.einsum(
                "grij,jgd->igrd", probs_b, value_blk, preferred_element_type=jnp.float32
            )

        out_acc = add_values()
    delta_rows = jnp.transpose(jnp.sum(grad_rows.astype(jnp.float32) * out_acc, axis=-1), (1, 2, 0))
    flat_zeros = jnp.zeros((tok_rows, kv_heads * DH), jnp.float32)
    query_zeros = jnp.zeros((tok_rows, kv_heads, q_group, DH), jnp.float32)

    def grad_parts(hop_count):
        block = blocks[hop_count]
        allowed = masks[hop_count]
        key_blk = block[0].reshape(tok_rows, kv_heads, DH)
        value_blk = block[1].reshape(tok_rows, kv_heads, DH)
        probs = probs_of(hop_count)
        probs_b = probs.astype(jnp.bfloat16)
        dprobs = jnp.einsum(
            "igrd,jgd->grij", grad_rows, value_blk, preferred_element_type=jnp.float32
        )
        dscores_b = (probs * (dprobs - delta_rows[..., None])).astype(jnp.bfloat16)
        query_part = jnp.einsum(
            "grij,jgd->igrd", dscores_b, key_blk, preferred_element_type=jnp.float32
        )
        key_part = (
            jnp.einsum("grij,igrd->jgd", dscores_b, query_rows, preferred_element_type=jnp.float32)
            * scaling
        )
        value_part = jnp.einsum(
            "grij,igrd->jgd", probs_b, grad_rows, preferred_element_type=jnp.float32
        )
        return (query_part, key_part.reshape(tok_rows, -1), value_part.reshape(tok_rows, -1))

    query_acc = query_zeros
    carried = (flat_zeros, flat_zeros)
    for hop_count in range(SPAN, 0, -1):
        query_part, key_part, value_part = grad_parts(hop_count)
        query_acc = query_acc + query_part
        carried = from_behind(
            (as_sent(carried[0] + key_part), as_sent(carried[1] + value_part)), "seq", -1
        )
    query_part, key_part, value_part = grad_parts(0)
    query_acc = query_acc + query_part
    key_sum = carried[0] + key_part
    value_sum = carried[1] + value_part
    key_grad, value_grad = (
        lax.psum_scatter(key_sum, "head", scatter_dimension=1, tiled=True),
        lax.psum_scatter(value_sum, "head", scatter_dimension=1, tiled=True),
    )
    attended = out_acc.reshape(tok_rows, QH * DH).astype(jnp.bfloat16)[None]
    query_grad = (query_acc * scaling).reshape(tok_rows, QH * DH).astype(jnp.bfloat16)[None]
    return (attended, query_grad, key_grad, value_grad)


def solution(mesh):
    placed = (
        P("head", "seq", None),
        P("seq", "head"),
        P("seq", "head"),
        P("head", "seq", None),
        P("seq"),
    )
    return jax.shard_map(
        shards,
        mesh=mesh,
        in_specs=placed,
        out_specs=(
            P("head", "seq", None),
            P("head", "seq", None),
            P("seq", "head"),
            P("seq", "head"),
        ),
        check_vma=False,
    )
```

profile of v0, /device:TPU:0, one launch (start us, length us, event | category | flops | bytes accessed | tf_op | source)
XLA Modules:
  0.0 220.8 jit_solution(3745732665473046738)
XLA Ops:
  7.2 5.0 %collective-permute-start = (s32[128]{0:T(128)}, s32[128]{0:T(128)S(1)}, u32[]{:S(2)}, u32[]{:S(2)}) collective-permute-start(s32[128]{0:T(128)} %param.9), channel_id=1, source_target_pairs={{0,1},{1,2},{2,3},{3,4},{4,5},{5,6},{6,7},{8,9},{9,10},{10,11},{11... | collective-permute-start | bytes 1544 | tf_op jit(solution)/shard_map/ppermute | solution.py:24
  12.2 5.7 %all_gather.7 = bf16[128,512]{1,0:T(8,128)(2,1)S(1)} all-gather(bf16[128,128]{1,0:T(8,128)(2,1)} %param.7), channel_id=1, replica_groups=mesh['head'=4,'seq'=8] {'head'}, dimensions={1}, use_global_device_ids=true | all-gather | bytes 163840 | tf_op jit(solution)/shard_map/all_gather | solution.py:30
  17.9 4.1 %collective-permute-start.8 = (bf16[128,512]{1,0:T(8,128)(2,1)S(1)}, bf16[128,512]{1,0:T(8,128)(2,1)}, u32[]{:S(2)}, u32[]{:S(2)}) collective-permute-start(bf16[128,512]{1,0:T(8,128)(2,1)S(1)} %all_gather.7), channel_id=1, source_target_pairs={{0,1},{1,2},{2,3},{3,4},{4,5},{5,6},{6,7},{8,9},{9,10},{10,11},{11... | collective-permute-start | bytes 393224 | tf_op jit(solution)/shard_map/ppermute | solution.py:24
  22.8 5.4 %all_gather.6 = bf16[128,512]{0,1:T(8,128)(2,1)S(1)} all-gather(bf16[128,128]{0,1:T(8,128)(2,1)S(1)} %copy.72), channel_id=1, replica_groups=mesh['head'=4,'seq'=8] {'head'}, dimensions={1}, use_global_device_ids=true | all-gather | bytes 163840 | tf_op jit(solution)/shard_map/all_gather | solution.py:29
  28.3 2.8 %collective-permute-start.1 = (bf16[128,512]{0,1:T(8,128)(2,1)S(1)}, bf16[128,512]{0,1:T(8,128)(2,1)S(1)}, u32[]{:S(2)}, u32[]{:S(2)}) collective-permute-start(bf16[128,512]{0,1:T(8,128)(2,1)S(1)} %all_gather.6), channel_id=1, source_target_pairs={{0,1},{1,2},{2,3},{3,4},{4,5},{5,6},{6,7},{8,9},{9,10},{10,11},{11... | collective-permute-start | bytes 393224 | tf_op jit(solution)/shard_map/ppermute | solution.py:24
  31.2 3.4 %collective-permute-start.2 = (s32[128]{0:T(128)S(1)}, s32[128]{0:T(128)S(1)}, u32[]{:S(2)}, u32[]{:S(2)}) collective-permute-start(s32[128]{0:T(128)S(1)} %collective-permute-done), channel_id=1, source_target_pairs={{0,1},{1,2},{2,3},{3,4},{4,5},{5,6},{6,7},{8,9},{9,10},{10,11},{11... | collective-permute-start | bytes 1544 | tf_op jit(solution)/shard_map/ppermute | solution.py:24
  34.6 1.3 collective-permute-done.2
  35.9 4.1 %collective-permute-start.4 = (s32[128]{0:T(128)S(1)}, s32[128]{0:T(128)S(1)}, u32[]{:S(2)}, u32[]{:S(2)}) collective-permute-start(s32[128]{0:T(128)S(1)} %collective-permute-done.2), channel_id=1, source_target_pairs={{0,1},{1,2},{2,3},{3,4},{4,5},{5,6},{6,7},{8,9},{9,10},{10,11},{11... | collective-permute-start | bytes 1544 | tf_op jit(solution)/shard_map/ppermute | solution.py:24
  40.0 1.3 collective-permute-done.4
  41.3 4.3 %collective-permute-start.6 = (s32[128]{0:T(128)S(1)}, s32[128]{0:T(128)S(1)}, u32[]{:S(2)}, u32[]{:S(2)}) collective-permute-start(s32[128]{0:T(128)S(1)} %collective-permute-done.4), channel_id=1, source_target_pairs={{0,1},{1,2},{2,3},{3,4},{4,5},{5,6},{6,7},{8,9},{9,10},{10,11},{11... | collective-permute-start | bytes 1544 | tf_op jit(solution)/shard_map/ppermute | solution.py:24
  45.8 1.6 copy.73
  47.4 1.3 copy.94
  50.6 5.0 %collective-permute-start.3 = (bf16[128,512]{0,1:T(8,128)(2,1)S(1)}, bf16[128,512]{0,1:T(8,128)(2,1)S(1)}, u32[]{:S(2)}, u32[]{:S(2)}) collective-permute-start(bf16[128,512]{0,1:T(8,128)(2,1)S(1)} %collective-permute-done.1), channel_id=1, source_target_pairs={{0,1},{1,2},{2,3},{3,4},{4,5},{5,6},{6,7},{8,9},{9,10},{10,11},{11... | collective-permute-start | bytes 393224 | tf_op jit(solution)/shard_map/ppermute | solution.py:24
  55.6 2.3 %fusion.13 = (f32[4,7,128]{2,1,0:T(8,128)}, f32[4,128,128,7]{2,1,3,0:T(8,128)}) fusion(pred[128,128]{0,1:T(8,128)(4,1)S(1)} %get-tuple-element.18, bf16[128,4,128,1]{0,2,3,1:T(8,128)(2,1)S(1)} %bitcast.350, bf16[128,4,7,128]{0,3,2,1:T(8,128)(2,1)S(1)} %bitcast.317), kind=kOutput, calls=%fused_computation.36 | convolution fusion | flops 118813184 | bytes 2914304 | tf_op jit(solution)/shard_map/igrd,jgd->grij/dot_general | solution.py:58
  58.0 1.7 copy.86
  59.6 3.9 %collective-permute-start.9 = (bf16[128,512]{1,0:T(8,128)(2,1)}, bf16[128,512]{1,0:T(8,128)(2,1)}, u32[]{:S(2)}, u32[]{:S(2)}) collective-permute-start(bf16[128,512]{1,0:T(8,128)(2,1)} %collective-permute-done.8), channel_id=1, source_target_pairs={{0,1},{1,2},{2,3},{3,4},{4,5},{5,6},{6,7},{8,9},{9,10},{10,11},{11... | collective-permute-start | bytes 393224 | tf_op jit(solution)/shard_map/ppermute | solution.py:24
  63.6 2.9 %collective-permute-start.5 = (bf16[128,512]{0,1:T(8,128)(2,1)S(1)}, bf16[128,512]{0,1:T(8,128)(2,1)S(1)}, u32[]{:S(2)}, u32[]{:S(2)}) collective-permute-start(bf16[128,512]{0,1:T(8,128)(2,1)S(1)} %collective-permute-done.3), channel_id=1, source_target_pairs={{0,1},{1,2},{2,3},{3,4},{4,5},{5,6},{6,7},{8,9},{9,10},{10,11},{11... | collective-permute-start | bytes 393224 | tf_op jit(solution)/shard_map/ppermute | solution.py:24
  66.5 2.3 %fusion.14 = (f32[4,7,128]{2,1,0:T(8,128)}, f32[4,128,128,7]{2,1,3,0:T(8,128)}) fusion(pred[128,128]{0,1:T(8,128)(4,1)S(1)} %get-tuple-element.19, bf16[128,4,128,1]{0,2,3,1:T(8,128)(2,1)S(1)} %bitcast.352, bf16[128,4,7,128]{0,3,2,1:T(8,128)(2,1)S(1)} %bitcast.318), kind=kOutput, calls=%fused_computation.37 | convolution fusion | flops 118813184 | bytes 2914304 | tf_op jit(solution)/shard_map/igrd,jgd->grij/dot_general | solution.py:58
  68.8 1.7 copy.88
  70.4 3.9 %collective-permute-start.10 = (bf16[128,512]{1,0:T(8,128)(2,1)}, bf16[128,512]{1,0:T(8,128)(2,1)}, u32[]{:S(2)}, u32[]{:S(2)}) collective-permute-start(bf16[128,512]{1,0:T(8,128)(2,1)} %collective-permute-done.9), channel_id=1, source_target_pairs={{0,1},{1,2},{2,3},{3,4},{4,5},{5,6},{6,7},{8,9},{9,10},{10,11},{11... | collective-permute-start | bytes 393224 | tf_op jit(solution)/shard_map/ppermute | solution.py:24
  74.4 1.9 collective-permute-start.7
  76.2 3.0 %fusion.15 = (f32[4,7,128]{2,1,0:T(8,128)}, f32[4,128,128,7]{2,1,3,0:T(8,128)}) fusion(pred[128,128]{0,1:T(8,128)(4,1)} %get-tuple-element.20, bf16[128,4,128,1]{0,2,3,1:T(8,128)(2,1)S(1)} %bitcast.354, bf16[128,4,7,128]{0,3,2,1:T(8,128)(2,1)S(1)} %bitcast.319), kind=kOutput, calls=%fused_computation.38 | convolution fusion | flops 118813184 | bytes 2914304 | tf_op jit(solution)/shard_map/igrd,jgd->grij/dot_general | solution.py:58
  79.2 1.7 copy.90
  80.9 3.2 %collective-permute-start.11 = (bf16[128,512]{1,0:T(8,128)(2,1)}, bf16[128,512]{1,0:T(8,128)(2,1)}, u32[]{:S(2)}, u32[]{:S(2)}) collective-permute-start(bf16[128,512]{1,0:T(8,128)(2,1)} %collective-permute-done.10), channel_id=1, source_target_pairs={{0,1},{1,2},{2,3},{3,4},{4,5},{5,6},{6,7},{8,9},{9,10},{10,11},{11... | collective-permute-start | bytes 393224 | tf_op jit(solution)/shard_map/ppermute | solution.py:24
  89.5 1.4 fusion.23
  90.8 1.4 fusion.27
  92.2 1.4 fusion.31
  93.6 1.4 fusion.35
  95.9 1.8 fusion.37
  97.7 1.8 fusion.33
  99.6 1.9 fusion.29
  101.5 1.7 fusion.46
  105.5 5.6 %bitcast_convert_fusion = (bf16[128,4,7,128]{0,3,2,1:T(8,128)(2,1)}, f32[4,7,128,128]{2,3,1,0:T(8,128)S(1)}) fusion(bf16[128,4,128,1]{0,2,3,1:T(8,128)(2,1)S(1)} %bitcast.348, f32[4,7,128]{2,1,0:T(8,128)} %copy-done.27, f32[4,7,128]{2,1,0:T(8,128)S(1)} %get-tuple-element.12, f32[4,128,128,7]{2,1,3,0:T(8,128)} %copy-done, pred[128,128]{0,1:T(8,128)(4,1)} %copy-done.15, ...), kind=kOutput, calls=%fused_computation.16 | convolution fusion | flops 122028032 | bytes 12103680 | tf_op jit(solution)/shard_map/grij,jgd->igrd/dot_general | solution.py:90
  112.6 1.7 fusion.7
  117.3 1.7 fusion.9
  118.9 1.8 fusion.1
  123.5 1.6 fusion.49
  125.9 1.4 collective-permute-start.16
  127.3 2.8 %fusion.47 = f32[4,7,128,128]{2,3,1,0:T(8,128)} fusion(bf16[128,4,128,1]{0,2,3,1:T(8,128)(2,1)S(1)} %bitcast.355, bf16[4,7,128,128]{2,3,1,0:T(8,128)(2,1)} %fusion.7), kind=kOutput, calls=%fused_computation.94 | convolution fusion | flops 117440512 | bytes 2883584 | tf_op jit(solution)/shard_map/grij,jgd->igrd/dot_general | solution.py:110
  133.2 1.6 add_convert_fusion.2
  134.8 1.3 collective-permute-start.17
  136.0 1.6 fusion.22
  137.7 1.8 copy.125
  142.2 1.3 collective-permute-start.12
  144.5 1.8 copy.113
  146.3 1.8 copy.115
  149.2 1.3 collective-permute-start.18
  151.5 1.3 collective-permute-start.13
  152.8 4.5 %collective-permute-done.18 = bf16[128,512]{1,0:T(8,128)(2,1)S(1)} collective-permute-done((bf16[128,512]{1,0:T(8,128)(2,1)S(1)}, bf16[128,512]{1,0:T(8,128)(2,1)S(1)}, u32[]{:S(2)}, u32[]{:S(2)}) %collective-permute-start.18) | collective-permute-done | bytes 131104 | tf_op jit(solution)/shard_map/ppermute | solution.py:24
  158.3 1.3 collective-permute-start.19
  160.6 1.6 add_convert_fusion.4
  162.2 1.3 collective-permute-start.14
  163.5 2.6 %collective-permute-done.19 = bf16[128,512]{1,0:T(8,128)(2,1)S(1)} collective-permute-done((bf16[128,512]{1,0:T(8,128)(2,1)S(1)}, bf16[128,512]{1,0:T(8,128)(2,1)S(1)}, u32[]{:S(2)}, u32[]{:S(2)}) %collective-permute-start.19) | collective-permute-done | bytes 131104 | tf_op jit(solution)/shard_map/ppermute | solution.py:24
  166.9 3.1 %collective-permute-done.14 = bf16[128,512]{1,0:T(8,128)(2,1)} collective-permute-done((bf16[128,512]{1,0:T(8,128)(2,1)}, bf16[128,512]{1,0:T(8,128)(2,1)}, u32[]{:S(2)}, u32[]{:S(2)}) %collective-permute-start.14) | collective-permute-done | bytes 131104 | tf_op jit(solution)/shard_map/ppermute | solution.py:24
  170.0 1.6 add_convert_fusion.3
  171.5 1.3 collective-permute-start.15
  172.8 1.6 fusion.21
  174.6 5.1 %collective-permute-done.15 = bf16[128,512]{1,0:T(8,128)(2,1)} collective-permute-done((bf16[128,512]{1,0:T(8,128)(2,1)}, bf16[128,512]{1,0:T(8,128)(2,1)}, u32[]{:S(2)}, u32[]{:S(2)}) %collective-permute-start.15) | collective-permute-done | bytes 131104 | tf_op jit(solution)/shard_map/ppermute | solution.py:24
  179.7 1.7 convert_add_fusion.1
  181.4 2.8 %fusion.50 = f32[4,7,128,128]{2,3,1,0:T(8,128)} fusion(bf16[128,4,128,1]{0,2,3,1:T(8,128)(2,1)S(1)} %bitcast.340, bf16[4,7,128,128]{2,3,1,0:T(8,128)(2,1)} %fusion.1), kind=kOutput, calls=%fused_computation.97 | convolution fusion | flops 117440512 | bytes 2883584 | tf_op jit(solution)/shard_map/grij,jgd->igrd/dot_general | solution.py:110
  184.2 1.3 copy.130
  185.5 3.6 %multiply_convert_fusion = bf16[4,7,128,128]{2,3,1,0:T(8,128)(2,1)S(1)} fusion(f32[4,7,128,128]{2,3,1,0:T(8,128)} %fusion.50, f32[4,7,128,128]{2,3,1,0:T(8,128)} %fusion.49, f32[4,7,128,128]{2,3,1,0:T(8,128)S(1)} %fusion.48, f32[4,7,128,128]{2,3,1,0:T(8,128)} %fusion.47, bf16[128,4,128,1]{0,2,3,1:T(8,128)(2,1)S(1)} %bitcast.347, ...), kind=kOutput, calls=%fused_computation.23 | convolution fusion | flops 120193024 | bytes 9306112 | tf_op jit(solution)/shard_map/grij,jgd->igrd/dot_general | solution.py:110
  189.1 1.3 copy.131
  190.7 23.2 %reduce-scatter.3.cloned.1.call-done = f32[128,128]{1,0:T(8,128)} async-done(((f32[128,512]{1,0:T(8,128)}), f32[128,128]{1,0:T(8,128)}) %reduce-scatter.3.cloned.1.call-update) | async-done | bytes 65552 | tf_op jit(solution)/shard_map/reduce_scatter | solution.py:135
  (138 shorter events, 31.5 us)
Async XLA Ops:
  7.2 40.2 %copy-start.12 = (bf16[1,128,3584]{2,1,0:T(8,128)(2,1)S(1)}, bf16[1,128,3584]{2,1,0:T(8,128)(2,1)}, u32[]{:S(2)}) copy-start(bf16[1,128,3584]{2,1,0:T(8,128)(2,1)} %param.8) | copy-start | bytes 2752516
  7.2 183.5 %reduce-scatter.5.cloned.1.call-start = ((), (), s32[]{:S(2)}) async-start(), calls=%async_computation.3 | async-start | bytes 327680 | tf_op jit(solution)/shard_map/reduce_scatter | solution.py:136
  7.2 23.9 %collective-permute-start = (s32[128]{0:T(128)}, s32[128]{0:T(128)S(1)}, u32[]{:S(2)}, u32[]{:S(2)}) collective-permute-start(s32[128]{0:T(128)} %param.9), channel_id=1, source_target_pairs={{0,1},{1,2},{2,3},{3,4},{4,5},{5,6},{6,7},{8,9},{9,10},{10,11},{11... | collective-permute-start | bytes 1544 | tf_op jit(solution)/shard_map/ppermute | solution.py:24
  17.9 40.1 %collective-permute-start.8 = (bf16[128,512]{1,0:T(8,128)(2,1)S(1)}, bf16[128,512]{1,0:T(8,128)(2,1)}, u32[]{:S(2)}, u32[]{:S(2)}) collective-permute-start(bf16[128,512]{1,0:T(8,128)(2,1)S(1)} %all_gather.7), channel_id=1, source_target_pairs={{0,1},{1,2},{2,3},{3,4},{4,5},{5,6},{6,7},{8,9},{9,10},{10,11},{11... | collective-permute-start | bytes 393224 | tf_op jit(solution)/shard_map/ppermute | solution.py:24
  28.3 22.3 %collective-permute-start.1 = (bf16[128,512]{0,1:T(8,128)(2,1)S(1)}, bf16[128,512]{0,1:T(8,128)(2,1)S(1)}, u32[]{:S(2)}, u32[]{:S(2)}) collective-permute-start(bf16[128,512]{0,1:T(8,128)(2,1)S(1)} %all_gather.6), channel_id=1, source_target_pairs={{0,1},{1,2},{2,3},{3,4},{4,5},{5,6},{6,7},{8,9},{9,10},{10,11},{11... | collective-permute-start | bytes 393224 | tf_op jit(solution)/shard_map/ppermute | solution.py:24
  31.2 4.7 %collective-permute-start.2 = (s32[128]{0:T(128)S(1)}, s32[128]{0:T(128)S(1)}, u32[]{:S(2)}, u32[]{:S(2)}) collective-permute-start(s32[128]{0:T(128)S(1)} %collective-permute-done), channel_id=1, source_target_pairs={{0,1},{1,2},{2,3},{3,4},{4,5},{5,6},{6,7},{8,9},{9,10},{10,11},{11... | collective-permute-start | bytes 1544 | tf_op jit(solution)/shard_map/ppermute | solution.py:24
  35.9 5.4 %collective-permute-start.4 = (s32[128]{0:T(128)S(1)}, s32[128]{0:T(128)S(1)}, u32[]{:S(2)}, u32[]{:S(2)}) collective-permute-start(s32[128]{0:T(128)S(1)} %collective-permute-done.2), channel_id=1, source_target_pairs={{0,1},{1,2},{2,3},{3,4},{4,5},{5,6},{6,7},{8,9},{9,10},{10,11},{11... | collective-permute-start | bytes 1544 | tf_op jit(solution)/shard_map/ppermute | solution.py:24
  41.3 7.4 %collective-permute-start.6 = (s32[128]{0:T(128)S(1)}, s32[128]{0:T(128)S(1)}, u32[]{:S(2)}, u32[]{:S(2)}) collective-permute-start(s32[128]{0:T(128)S(1)} %collective-permute-done.4), channel_id=1, source_target_pairs={{0,1},{1,2},{2,3},{3,4},{4,5},{5,6},{6,7},{8,9},{9,10},{10,11},{11... | collective-permute-start | bytes 1544 | tf_op jit(solution)/shard_map/ppermute | solution.py:24
  45.8 55.8 %copy-start.13 = (bf16[128,512]{0,1:T(8,128)(2,1)}, bf16[128,512]{0,1:T(8,128)(2,1)S(1)}, u32[]{:S(2)}) copy-start(bf16[128,512]{0,1:T(8,128)(2,1)S(1)} %copy.84) | copy-start | bytes 393220
  45.8 2.9 %copy-start.40 = (s32[128]{0:T(128)S(1)}, s32[128]{0:T(128)}, u32[]{:S(2)}) copy-start(s32[128]{0:T(128)} %param.9) | copy-start | bytes 1540
  49.5 8.4 %copy-start.19 = (pred[128,128]{0,1:T(8,128)(4,1)}, pred[128,128]{0,1:T(8,128)(4,1)S(1)}, u32[]{:S(2)}) copy-start(pred[128,128]{0,1:T(8,128)(4,1)S(1)} %get-tuple-element.18) | copy-start | bytes 49156
  49.5 17.0 %copy-start.22 = (pred[128,128]{0,1:T(8,128)(4,1)}, pred[128,128]{0,1:T(8,128)(4,1)S(1)}, u32[]{:S(2)}) copy-start(pred[128,128]{0,1:T(8,128)(4,1)S(1)} %get-tuple-element.19) | copy-start | bytes 49156
  49.5 34.5 %copy-start.15 = (pred[128,128]{0,1:T(8,128)(4,1)}, pred[128,128]{0,1:T(8,128)(4,1)S(1)}, u32[]{:S(2)}) copy-start(pred[128,128]{0,1:T(8,128)(4,1)S(1)} %get-tuple-element.21) | copy-start | bytes 49156
  50.6 13.0 %collective-permute-start.3 = (bf16[128,512]{0,1:T(8,128)(2,1)S(1)}, bf16[128,512]{0,1:T(8,128)(2,1)S(1)}, u32[]{:S(2)}, u32[]{:S(2)}) collective-permute-start(bf16[128,512]{0,1:T(8,128)(2,1)S(1)} %collective-permute-done.1), channel_id=1, source_target_pairs={{0,1},{1,2},{2,3},{3,4},{4,5},{5,6},{6,7},{8,9},{9,10},{10,11},{11... | collective-permute-start | bytes 393224 | tf_op jit(solution)/shard_map/ppermute | solution.py:24
  59.6 9.2 %collective-permute-start.9 = (bf16[128,512]{1,0:T(8,128)(2,1)}, bf16[128,512]{1,0:T(8,128)(2,1)}, u32[]{:S(2)}, u32[]{:S(2)}) collective-permute-start(bf16[128,512]{1,0:T(8,128)(2,1)} %collective-permute-done.8), channel_id=1, source_target_pairs={{0,1},{1,2},{2,3},{3,4},{4,5},{5,6},{6,7},{8,9},{9,10},{10,11},{11... | collective-permute-start | bytes 393224 | tf_op jit(solution)/shard_map/ppermute | solution.py:24
  63.6 10.8 %collective-permute-start.5 = (bf16[128,512]{0,1:T(8,128)(2,1)S(1)}, bf16[128,512]{0,1:T(8,128)(2,1)S(1)}, u32[]{:S(2)}, u32[]{:S(2)}) collective-permute-start(bf16[128,512]{0,1:T(8,128)(2,1)S(1)} %collective-permute-done.3), channel_id=1, source_target_pairs={{0,1},{1,2},{2,3},{3,4},{4,5},{5,6},{6,7},{8,9},{9,10},{10,11},{11... | collective-permute-start | bytes 393224 | tf_op jit(solution)/shard_map/ppermute | solution.py:24
  70.4 8.8 %collective-permute-start.10 = (bf16[128,512]{1,0:T(8,128)(2,1)}, bf16[128,512]{1,0:T(8,128)(2,1)}, u32[]{:S(2)}, u32[]{:S(2)}) collective-permute-start(bf16[128,512]{1,0:T(8,128)(2,1)} %collective-permute-done.9), channel_id=1, source_target_pairs={{0,1},{1,2},{2,3},{3,4},{4,5},{5,6},{6,7},{8,9},{9,10},{10,11},{11... | collective-permute-start | bytes 393224 | tf_op jit(solution)/shard_map/ppermute | solution.py:24
  74.4 9.7 %collective-permute-start.7 = (bf16[128,512]{0,1:T(8,128)(2,1)S(1)}, bf16[128,512]{0,1:T(8,128)(2,1)S(1)}, u32[]{:S(2)}, u32[]{:S(2)}) collective-permute-start(bf16[128,512]{0,1:T(8,128)(2,1)S(1)} %collective-permute-done.5), channel_id=1, source_target_pairs={{0,1},{1,2},{2,3},{3,4},{4,5},{5,6},{6,7},{8,9},{9,10},{10,11},{11... | collective-permute-start | bytes 393224 | tf_op jit(solution)/shard_map/ppermute | solution.py:24
  80.9 3.7 %copy-start.29 = (f32[4,7,128]{2,1,0:T(8,128)S(1)}, f32[4,7,128]{2,1,0:T(8,128)}, u32[]{:S(2)}) copy-start(f32[4,7,128]{2,1,0:T(8,128)} %get-tuple-element.30) | copy-start | bytes 43012
  80.9 3.7 %copy-start.37 = (f32[4,7,128]{2,1,0:T(8,128)S(1)}, f32[4,7,128]{2,1,0:T(8,128)}, u32[]{:S(2)}) copy-start(f32[4,7,128]{2,1,0:T(8,128)} %get-tuple-element.28) | copy-start | bytes 43012
  80.9 3.7 %copy-start.38 = (f32[4,7,128]{2,1,0:T(8,128)S(1)}, f32[4,7,128]{2,1,0:T(8,128)}, u32[]{:S(2)}) copy-start(f32[4,7,128]{2,1,0:T(8,128)} %get-tuple-element.26) | copy-start | bytes 43012
  80.9 3.7 %copy-start.39 = (f32[4,7,128]{2,1,0:T(8,128)S(1)}, f32[4,7,128]{2,1,0:T(8,128)}, u32[]{:S(2)}) copy-start(f32[4,7,128]{2,1,0:T(8,128)} %get-tuple-element.24) | copy-start | bytes 43012
  80.9 23.5 %collective-permute-start.11 = (bf16[128,512]{1,0:T(8,128)(2,1)}, bf16[128,512]{1,0:T(8,128)(2,1)}, u32[]{:S(2)}, u32[]{:S(2)}) collective-permute-start(bf16[128,512]{1,0:T(8,128)(2,1)} %collective-permute-done.10), channel_id=1, source_target_pairs={{0,1},{1,2},{2,3},{3,4},{4,5},{5,6},{6,7},{8,9},{9,10},{10,11},{11... | collective-permute-start | bytes 393224 | tf_op jit(solution)/shard_map/ppermute | solution.py:24
  84.1 1.6 copy-start.6
  84.1 2.7 %copy-start.8 = (f32[4,128,128,7]{2,1,3,0:T(8,128)S(1)}, f32[4,128,128,7]{2,1,3,0:T(8,128)}, u32[]{:S(2)}) copy-start(f32[4,128,128,7]{2,1,3,0:T(8,128)} %get-tuple-element.25) | copy-start | bytes 5505028
  84.1 2.7 %copy-start.23 = (pred[128,128]{0,1:T(8,128)(4,1)S(1)}, pred[128,128]{0,1:T(8,128)(4,1)}, u32[]{:S(2)}) copy-start(pred[128,128]{0,1:T(8,128)(4,1)} %copy-done.22) | copy-start | bytes 49156
  84.1 2.7 %copy-start.25 = (pred[128,128]{0,1:T(8,128)(4,1)S(1)}, pred[128,128]{0,1:T(8,128)(4,1)}, u32[]{:S(2)}) copy-start(pred[128,128]{0,1:T(8,128)(4,1)} %get-tuple-element.20) | copy-start | bytes 49156
  84.6 4.8 %copy-start = (f32[4,128,128,7]{2,1,3,0:T(8,128)}, f32[4,128,128,7]{2,1,3,0:T(8,128)S(1)}, u32[]{:S(2)}) copy-start(f32[4,128,128,7]{2,1,3,0:T(8,128)S(1)} %get-tuple-element.23) | copy-start | bytes 5505028
  86.8 1.5 copy-start.4
  86.8 1.5 copy-start.16
  86.8 1.5 copy-start.20
  88.3 1.2 copy-start.2
  89.3 10.2 %copy-start.27 = (f32[4,7,128]{2,1,0:T(8,128)}, f32[4,7,128]{2,1,0:T(8,128)S(1)}, u32[]{:S(2)}) copy-start(f32[4,7,128]{2,1,0:T(8,128)S(1)} %multiply_add_fusion) | copy-start | bytes 43012
  95.0 0.9 copy-start.30
  95.9 1.8 copy-start.32
  97.7 1.9 copy-start.34
  105.4 5.6 %copy-start.3 = (bf16[1,128,3584]{1,2,0:T(8,128)(2,1)S(1)}, bf16[1,128,3584]{1,2,0:T(8,128)(2,1)}, u32[]{:S(2)}) copy-start(bf16[1,128,3584]{1,2,0:T(8,128)(2,1)} %copy.94) | copy-start | bytes 2752516
  111.0 1.5 copy-start.9
  111.0 1.5 copy-start.26
  111.0 1.5 copy-start.28
  111.0 1.5 copy-start.35
  112.5 1.7 copy-start.7
  112.5 1.7 copy-start.24
  112.6 1.7 copy-start.33
  114.2 1.5 copy-start.5
  114.3 1.5 copy-start.21
  114.3 1.5 copy-start.31
  115.8 1.5 copy-start.1
  115.8 1.5 copy-start.17
  117.3 1.7 copy-start.14
  123.5 1.6 copy-start.36
  125.9 4.2 %copy-start.11 = (bf16[4,7,128,128]{2,3,1,0:T(8,128)(2,1)S(1)}, bf16[4,7,128,128]{2,3,1,0:T(8,128)(2,1)}, u32[]{:S(2)}) copy-start(bf16[4,7,128,128]{2,3,1,0:T(8,128)(2,1)} %fusion.7) | copy-start | bytes 2752516
  125.9 7.3 %collective-permute-start.16 = (bf16[128,512]{1,0:T(8,128)(2,1)}, bf16[128,512]{1,0:T(8,128)(2,1)}, u32[]{:S(2)}, u32[]{:S(2)}) collective-permute-start(bf16[128,512]{1,0:T(8,128)(2,1)} %copy.121), channel_id=1, source_target_pairs={{1,0},{2,1},{3,2},{4,3},{5,4},{6,5},{7,6},{9,8},{10,9},{11,10},{12... | collective-permute-start | bytes 393224 | tf_op jit(solution)/shard_map/ppermute | solution.py:24
  131.3 8.2 %copy-start.18 = (f32[4,128,128,1]{1,2,3,0:T(8,128)S(1)}, f32[4,128,128,1]{1,2,3,0:T(8,128)}, u32[]{:S(2)}) copy-start(f32[4,128,128,1]{1,2,3,0:T(8,128)} %fusion.35) | copy-start | bytes 786436
  134.8 13.4 %collective-permute-start.17 = (bf16[128,512]{1,0:T(8,128)(2,1)}, bf16[128,512]{1,0:T(8,128)(2,1)}, u32[]{:S(2)}, u32[]{:S(2)}) collective-permute-start(bf16[128,512]{1,0:T(8,128)(2,1)} %add_convert_fusion.2), channel_id=1, source_target_pairs={{1,0},{2,1},{3,2},{4,3},{5,4},{6,5},{7,6},{9,8},{10,9},{11,10},{12... | collective-permute-start | bytes 393224 | tf_op jit(solution)/shard_map/ppermute | solution.py:24
  142.2 8.3 %collective-permute-start.12 = (bf16[128,512]{1,0:T(8,128)(2,1)}, bf16[128,512]{1,0:T(8,128)(2,1)}, u32[]{:S(2)}, u32[]{:S(2)}) collective-permute-start(bf16[128,512]{1,0:T(8,128)(2,1)} %copy.111), channel_id=1, source_target_pairs={{1,0},{2,1},{3,2},{4,3},{5,4},{6,5},{7,6},{9,8},{10,9},{11,10},{12... | collective-permute-start | bytes 393224 | tf_op jit(solution)/shard_map/ppermute | solution.py:24
  149.2 8.1 %collective-permute-start.18 = (bf16[128,512]{1,0:T(8,128)(2,1)S(1)}, bf16[128,512]{1,0:T(8,128)(2,1)S(1)}, u32[]{:S(2)}, u32[]{:S(2)}) collective-permute-start(bf16[128,512]{1,0:T(8,128)(2,1)S(1)} %add_convert_fusion.1), channel_id=1, source_target_pairs={{1,0},{2,1},{3,2},{4,3},{5,4},{6,5},{7,6},{9,8},{10,9},{11,10},{12... | collective-permute-start | bytes 393224 | tf_op jit(solution)/shard_map/ppermute | solution.py:24
  151.5 9.1 %collective-permute-start.13 = (bf16[128,512]{1,0:T(8,128)(2,1)S(1)}, bf16[128,512]{1,0:T(8,128)(2,1)S(1)}, u32[]{:S(2)}, u32[]{:S(2)}) collective-permute-start(bf16[128,512]{1,0:T(8,128)(2,1)S(1)} %add_convert_fusion.5), channel_id=1, source_target_pairs={{1,0},{2,1},{3,2},{4,3},{5,4},{6,5},{7,6},{9,8},{10,9},{11,10},{12... | collective-permute-start | bytes 393224 | tf_op jit(solution)/shard_map/ppermute | solution.py:24
  158.3 7.8 %collective-permute-start.19 = (bf16[128,512]{1,0:T(8,128)(2,1)S(1)}, bf16[128,512]{1,0:T(8,128)(2,1)S(1)}, u32[]{:S(2)}, u32[]{:S(2)}) collective-permute-start(bf16[128,512]{1,0:T(8,128)(2,1)S(1)} %add_convert_fusion), channel_id=1, source_target_pairs={{1,0},{2,1},{3,2},{4,3},{5,4},{6,5},{7,6},{9,8},{10,9},{11,10},{12... | collective-permute-start | bytes 393224 | tf_op jit(solution)/shard_map/ppermute | solution.py:24
  162.2 7.8 %collective-permute-start.14 = (bf16[128,512]{1,0:T(8,128)(2,1)}, bf16[128,512]{1,0:T(8,128)(2,1)}, u32[]{:S(2)}, u32[]{:S(2)}) collective-permute-start(bf16[128,512]{1,0:T(8,128)(2,1)} %add_convert_fusion.4), channel_id=1, source_target_pairs={{1,0},{2,1},{3,2},{4,3},{5,4},{6,5},{7,6},{9,8},{10,9},{11,10},{12... | collective-permute-start | bytes 393224 | tf_op jit(solution)/shard_map/ppermute | solution.py:24
  166.8 47.1 %reduce-scatter.3.cloned.1.call-start = ((), (), s32[]{:S(2)}) async-start(), calls=%async_computation.2 | async-start | bytes 327680 | tf_op jit(solution)/shard_map/reduce_scatter | solution.py:135
  171.5 8.2 %collective-permute-start.15 = (bf16[128,512]{1,0:T(8,128)(2,1)}, bf16[128,512]{1,0:T(8,128)(2,1)}, u32[]{:S(2)}, u32[]{:S(2)}) collective-permute-start(bf16[128,512]{1,0:T(8,128)(2,1)} %add_convert_fusion.3), channel_id=1, source_target_pairs={{1,0},{2,1},{3,2},{4,3},{5,4},{6,5},{7,6},{9,8},{10,9},{11,10},{12... | collective-permute-start | bytes 393224 | tf_op jit(solution)/shard_map/ppermute | solution.py:24
  174.6 9.6 %copy-start.10 = (bf16[128,4,7,128]{0,3,2,1:T(8,128)(2,1)S(1)}, bf16[128,4,7,128]{0,3,2,1:T(8,128)(2,1)}, u32[]{:S(2)}) copy-start(bf16[128,4,7,128]{0,3,2,1:T(8,128)(2,1)} %get-tuple-element.32) | copy-start | bytes 2752516
Sparse Core Ops, SparseCore 0:
  166.9 23.7 reduce-scatter.4
  193.9 20.0 reduce-scatter.2
where the time goes:
time: 222 us; the launch traced here: 221 us
  starting transfers between devices  55 us (25%)
  matrix products  53.3 us (24%)
  waiting for transfers between devices  43.2 us (19%)
  local copies, waits for them, and re-layouts  29.4 us (13%)
  between operations  14.7 us (7%)
  other arithmetic  14 us (6%)
  blocking collectives  11.1 us (5%)
    ppermute x20, starting transfers between devices, from_behind(): lax.ppermute(value, axis, [(source, source + steps) for source in range(l...  55 us
    reduce_scatter x1, waiting for transfers between devices, shards(): lax.psum_scatter(key_sum, 'head', scatter_dimension=1, tiled=True)  23.2 us
    ppermute x20, waiting for transfers between devices, from_behind(): lax.ppermute(value, axis, [(source, source + steps) for source in range(l...  19.6 us
    dot_general x5, matrix products, add_values(): jnp.einsum('grij,jgd->igrd', probs_b, value_blk, preferred_element_type=j...  12.9 us
    unnamed x87, local copies, waits for them, and re-layouts  12.1 us
    dot_general x5, matrix products, grad_parts(): jnp.einsum('grij,jgd->igrd', dscores_b, key_blk, preferred_element_type=j...  11.2 us
    dot_general x5, matrix products, scores_of(): jnp.einsum('igrd,jgd->grij', query_rows, key_blk, preferred_element_type=...  9.12 us
    convert_element_type x6, other arithmetic, short(): return part.astype(jnp.bfloat16) if part.dtype == jnp.float32 else part  7.8 us
  transfers between devices with their start and end apart: 22, of which 10 were waited for; matrix products, arithmetic and copies ran while one was open for 32% of the time, Pallas kernels for 0%

commit v1 on v0

v1 whole, which is shorter than its diff:
```python
import functools
import math

import jax
import jax.numpy as jnp
from jax import lax
from jax.experimental import pallas as pl
from jax.experimental.pallas import tpu as pltpu
from jax.sharding import PartitionSpec as P

DH = 128
SPAN = 4
HOPS = SPAN + 1
BLOCK_ORDER = (1, 2, 3, 0, 4)
MESH = pl.DeviceIdType.MESH
NT = (((1,), (1,)), ((), ()))
NN = (((1,), (0,)), ((), ()))
TN = (((0,), (0,)), ((), ()))


def dot(a, b, dims):
    return lax.dot_general(a, b, dims, preferred_element_type=jnp.float32)


def kernel(
    seq_count, heads, group_size,
    q_hbm, k_ref, v_ref, g_hbm, seg_ref,
    out_hbm, dq_hbm, dk_ref, dv_ref,
    kv, qbuf, gbuf, obuf, dqbuf, kc, vc, bias, pscr, dscr,
    grad_own, grad_send, grad_recv, seq_send, seq_recv,
    in_sem, out_sem, kv_recv, kv_seq_send, kv_head_send,
    gr_send, gr_recv, sq_send, sq_recv,
):
    m = lax.axis_index("head")
    s = lax.axis_index("seq")
    rows = k_ref.shape[0]
    slab = group_size * DH
    scaling = 1.0 / math.sqrt(DH)
    core_peer = m + 1 - 2 * (m % 2)
    x_peer = (m + 2) % heads
    both_peer = (core_peer + 2) % heads
    groups = (m, core_peer, x_peer, both_peer)

    def columns(slot):
        return pl.ds(pl.multiple_of(groups[slot] * slab, DH), slab)

    def load(slot, which):
        src, dst = ((q_hbm, qbuf), (g_hbm, gbuf))[which]
        return pltpu.make_async_copy(
            src.at[0, :, columns(slot)], dst.at[slot], in_sem.at[which, slot])

    def store(slot, which):
        src, dst = ((obuf, out_hbm), (dqbuf, dq_hbm))[which]
        return pltpu.make_async_copy(
            src.at[slot], dst.at[0, :, columns(slot)], out_sem.at[which, slot])

    def remote(src, dst, send, recv, head, seq):
        return pltpu.make_async_remote_copy(
            src_ref=src, dst_ref=dst, send_sem=send, recv_sem=recv,
            device_id=(head, seq), device_id_type=MESH)

    def kv_seq(src_hop, dst_hop):
        return remote(kv.at[0, src_hop], kv.at[0, dst_hop], kv_seq_send.at[dst_hop],
                      kv_recv.at[0, dst_hop], m, s + (dst_hop - src_hop))

    def kv_head(slot, hop):
        src = kv.at[2 if slot == 3 else 0, hop]
        return remote(src, kv.at[slot, hop], kv_head_send.at[slot, hop],
                      kv_recv.at[slot, hop], x_peer if slot == 2 else core_peer, s)

    def kv_arrived(slot, hop):
        kv_head(slot, hop).wait_recv()

    for slot in (0, 1, 2, 3):
        load(slot, 0).start()
        load(slot, 1).start()

    kv[0, 0, 0:rows, :] = k_ref[...]
    kv[0, 0, rows:2 * rows, :] = v_ref[...]
    kv[0, 0, 2 * rows:, :] = jnp.broadcast_to(
        seg_ref[...].astype(jnp.float32), (16, rows)).astype(jnp.bfloat16)

    barrier = pltpu.get_barrier_semaphore()
    for peer in (core_peer, x_peer):
        pl.semaphore_signal(barrier, inc=1, device_id=(peer, s), device_id_type=MESH)
    expected = 2
    for step in (-2, -1, 1, 2):
        valid = (s >= -step) if step < 0 else (s < seq_count - step)

        @pl.when(valid)
        def _(step=step):
            pl.semaphore_signal(barrier, inc=1, device_id=(m, s + step), device_id_type=MESH)
        expected = expected + jnp.where(valid, 1, 0)
    pl.semaphore_wait(barrier, expected)

    for hop in (1, 2):
        @pl.when(s < seq_count - hop)
        def _(hop=hop):
            kv_seq(0, hop).start()
    kv_head(2, 0).start()
    kv_head(1, 0).start()

    for hop in range(1, HOPS):
        src_hop = hop if hop <= 2 else hop - 2

        @pl.when(s < hop)
        def _(hop=hop):
            kv[0, hop, 0:2 * rows, :] = jnp.zeros((2 * rows, DH), jnp.bfloat16)
            kv[0, hop, 2 * rows:, :] = jnp.full((16, DH), -1.0, jnp.bfloat16)

        @pl.when(s >= hop)
        def _(hop=hop):
            kv_seq(0 if hop <= 2 else hop - 2, hop).wait_recv()

        if hop <= 2:
            @pl.when((s >= hop) & (s < seq_count - 2))
            def _(hop=hop):
                kv_seq(hop, hop + 2).start()
        kv_head(2, hop).start()
        kv_head(1, hop).start()
        if hop >= 3:
            kv_arrived(2, hop - 3)
            kv_head(3, hop - 3).start()

    row_id = lax.broadcasted_iota(jnp.int32, (rows, rows), 0)
    col_id = lax.broadcasted_iota(jnp.int32, (rows, rows), 1)
    tri = col_id <= row_id

    def seg_row(hop):
        full = kv[0, hop, 2 * rows:, :].astype(jnp.float32)
        return full[0:1, :]

    seg_q = jnp.sum(jnp.where(row_id == col_id, seg_row(0), 0.0), axis=1, keepdims=True)
    for at, hop in enumerate((1, 2, 3)):
        bias[:, at * rows:(at + 1) * rows] = jnp.where(seg_row(hop) == seg_q, 0.0, -1e30)
    bias[:, 3 * rows:] = jnp.where(
        jnp.where(tri, seg_row(0), seg_row(4)) == seg_q, 0.0, -1e30)

    shared = 3 * rows

    def fold(x):
        edge = jnp.where(tri, x[:, shared:shared + rows], x[:, shared + rows:])
        return jnp.concatenate([x[:, :shared], edge], axis=1)

    def unfold(x):
        edge = x[:, shared:]
        zero = jnp.zeros_like(edge)
        return jnp.concatenate(
            [x[:, :shared], jnp.where(tri, edge, zero), jnp.where(tri, zero, edge)],
            axis=1).astype(jnp.bfloat16)

    def compute(slot):
        load(slot, 0).wait()
        load(slot, 1).wait()
        for at, hop in enumerate(BLOCK_ORDER):
            kc[at * rows:(at + 1) * rows, :] = kv[slot, hop, 0:rows, :]
            vc[at * rows:(at + 1) * rows, :] = kv[slot, hop, rows:2 * rows, :]

        for r in range(group_size):
            cols = slice(r * DH, (r + 1) * DH)
            q = qbuf[slot, :, cols]
            g = gbuf[slot, :, cols]
            t = fold(dot(q, kc[...], NT)) * (scaling * math.log2(math.e)) + bias[...]
            e = jnp.exp2(t - jnp.max(t, axis=1, keepdims=True))
            probs = e * (1.0 / jnp.sum(e, axis=1, keepdims=True))
            probs_b = unfold(probs)
            pscr[r * rows:(r + 1) * rows, :] = probs_b
            out32 = dot(probs_b, vc[...], NN)
            obuf[slot, :, cols] = out32.astype(jnp.bfloat16)
            delta = jnp.sum(g.astype(jnp.float32) * out32, axis=1, keepdims=True)
            dprobs = fold(dot(g, vc[...], NT))
            dscores_b = unfold(probs * (dprobs - delta))
            dscr[r * rows:(r + 1) * rows, :] = dscores_b
            dqbuf[slot, :, cols] = (dot(dscores_b, kc[...], NN) * scaling).astype(jnp.bfloat16)
        store(slot, 0).start()
        store(slot, 1).start()
        q_rows = jnp.concatenate(
            [qbuf[slot, :, r * DH:(r + 1) * DH] for r in range(group_size)], axis=0)
        g_rows = jnp.concatenate(
            [gbuf[slot, :, r * DH:(r + 1) * DH] for r in range(group_size)], axis=0)
        key_t = dot(q_rows, dscr[...], TN) * scaling
        value_t = dot(g_rows, pscr[...], TN)
        for at, hop in enumerate(BLOCK_ORDER):
            cols = slice(at * rows, (at + 1) * rows)
            if slot == 0:
                grad_own[hop, 0:DH, :] = key_t[:, cols]
                grad_own[hop, DH:, :] = value_t[:, cols]
            else:
                grad_send[slot - 1, hop, 0:DH, :] = key_t[:, cols].astype(jnp.bfloat16)
                grad_send[slot - 1, hop, DH:, :] = value_t[:, cols].astype(jnp.bfloat16)

    def gr_copy(slot):
        return remote(grad_send.at[slot - 1], grad_recv.at[slot - 1], gr_send.at[slot - 1],
                      gr_recv.at[slot - 1], x_peer if slot == 2 else core_peer, s)

    compute(0)
    for hop in (2, 3, 4):
        kv_arrived(2, hop)
        kv_head(3, hop).start()
    for hop in range(HOPS):
        kv_arrived(3, hop)
    compute(3)
    gr_copy(3).start()
    compute(2)
    gr_copy(3).wait_recv()
    grad_send[1] = (grad_send[1].astype(jnp.float32)
                    + grad_recv[2].astype(jnp.float32)).astype(jnp.bfloat16)
    gr_copy(2).start()
    for hop in range(HOPS):
        kv_arrived(1, hop)
    compute(1)
    gr_copy(1).start()
    gr_copy(1).wait_recv()
    gr_copy(2).wait_recv()

    def total(hop):
        return (grad_own[hop] + grad_recv[0, hop].astype(jnp.float32)
                + grad_recv[1, hop].astype(jnp.float32))

    def sq_copy(hop):
        return remote(seq_send.at[hop - 1], seq_recv.at[hop - 1], sq_send.at[hop - 1],
                      sq_recv.at[hop - 1], m, s - (hop if hop <= 2 else 2))

    for hop in (4, 3):
        @pl.when(s >= hop)
        def _(hop=hop):
            seq_send[hop - 1] = total(hop).astype(jnp.bfloat16)
            sq_copy(hop).start()
    for hop in (2, 1):
        grad_own[hop] = total(hop)

        @pl.when((s >= hop) & (s < seq_count - 2))
        def _(hop=hop):
            sq_copy(hop + 2).wait_recv()
            grad_own[hop] = grad_own[hop] + seq_recv[hop + 1].astype(jnp.float32)

        @pl.when(s >= hop)
        def _(hop=hop):
            seq_send[hop - 1] = grad_own[hop].astype(jnp.bfloat16)
            sq_copy(hop).start()
    grad_own[0] = total(0)
    for hop in (2, 1):
        @pl.when(s < seq_count - hop)
        def _(hop=hop):
            sq_copy(hop).wait_recv()
            grad_own[0] = grad_own[0] + seq_recv[hop - 1].astype(jnp.float32)
    dk_ref[...] = grad_own[0, 0:DH, :].T
    dv_ref[...] = grad_own[0, DH:, :].T

    for slot in (0, 1, 2, 3):
        store(slot, 0).wait()
        store(slot, 1).wait()
    for hop in (1, 2):
        @pl.when(s < seq_count - hop)
        def _(hop=hop):
            kv_seq(0, hop).wait_send()

        @pl.when((s >= hop) & (s < seq_count - 2))
        def _(hop=hop):
            kv_seq(hop, hop + 2).wait_send()
    for slot in (1, 2, 3):
        for hop in range(HOPS):
            kv_head(slot, hop).wait_send()
        gr_copy(slot).wait_send()
    for hop in range(1, HOPS):
        @pl.when(s >= hop)
        def _(hop=hop):
            sq_copy(hop).wait_send()


def shards(queries, trunk_keys, trunk_values, out_grad, segment_ids):
    rows = trunk_keys.shape[0]
    width = queries.shape[2]
    heads = lax.axis_size("head")
    seq_count = lax.axis_size("seq")
    group_size = width // (DH * heads)
    slab = group_size * DH
    vmem = pl.BlockSpec(memory_space=pltpu.VMEM)
    hbm = pl.BlockSpec(memory_space=pl.ANY)
    bf16, f32 = jnp.bfloat16, jnp.float32
    dma = pltpu.SemaphoreType.DMA
    big = jax.ShapeDtypeStruct(queries.shape, bf16)
    small = jax.ShapeDtypeStruct(trunk_keys.shape, f32)
    return tuple(pl.pallas_call(
        functools.partial(kernel, seq_count, heads, group_size),
        out_shape=(big, big, small, small),
        in_specs=[hbm, vmem, vmem, hbm, vmem],
        out_specs=(hbm, hbm, vmem, vmem),
        scratch_shapes=[
            pltpu.VMEM((heads, HOPS, 2 * rows + 16, DH), bf16),
            pltpu.VMEM((heads, rows, slab), bf16),
            pltpu.VMEM((heads, rows, slab), bf16),
            pltpu.VMEM((heads, rows, slab), bf16),
            pltpu.VMEM((heads, rows, slab), bf16),
            pltpu.VMEM((HOPS * rows, DH), bf16),
            pltpu.VMEM((HOPS * rows, DH), bf16),
            pltpu.VMEM((rows, SPAN * rows), f32),
            pltpu.VMEM((group_size * rows, HOPS * rows), bf16),
            pltpu.VMEM((group_size * rows, HOPS * rows), bf16),
            pltpu.VMEM((HOPS, 2 * DH, rows), f32),
            pltpu.VMEM((3, HOPS, 2 * DH, rows), bf16),
            pltpu.VMEM((3, HOPS, 2 * DH, rows), bf16),
            pltpu.VMEM((SPAN, 2 * DH, rows), bf16),
            pltpu.VMEM((SPAN, 2 * DH, rows), bf16),
            dma((2, heads)), dma((2, heads)),
            dma((heads, HOPS)), dma((HOPS,)), dma((heads, HOPS)),
            dma((3,)), dma((3,)), dma((SPAN,)), dma((SPAN,)),
        ],
        compiler_params=pltpu.CompilerParams(
            collective_id=0, has_side_effects=True, vmem_limit_bytes=40 * 1024 * 1024),
        cost_estimate=pl.CostEstimate(
            flops=12 * rows * rows * HOPS * width, bytes_accessed=8 * rows * width,
            transcendentals=rows * rows * HOPS * width // DH),
    )(queries, trunk_keys, trunk_values, out_grad, segment_ids.reshape(1, rows)))


def solution(mesh):
    placed = (
        P("head", "seq", None),
        P("seq", "head"),
        P("seq", "head"),
        P("head", "seq", None),
        P("seq"),
    )
    return jax.shard_map(
        shards,
        mesh=mesh,
        in_specs=placed,
        out_specs=(
            P("head", "seq", None),
            P("head", "seq", None),
            P("seq", "head"),
            P("seq", "head"),
        ),
        check_vma=False,
    )
```

time: 222 us -> 54.8 us (0.25)
  starting transfers between devices: 55 us -> 0 us
  matrix products: 53.3 us -> 0 us
  Pallas kernels: 0 us -> 46.2 us
  waiting for transfers between devices: 43.2 us -> 0 us
  local copies, waits for them, and re-layouts: 29.4 us -> 7.63 us
  between operations: 14.7 us -> 0.65 us
  other arithmetic: 14 us -> 0 us
  blocking collectives: 11.1 us -> 0 us
    ppermute x20 -> x0, starting transfers between devices: 55 us -> none  [from_behind(): lax.ppermute(value, axis, [(source, source + steps) for source in range(l...]
    dot_general x30 -> x0, matrix products: 53.3 us -> none  [the longest x5 12.9 us: add_values(): jnp.einsum('grij,jgd->igrd', probs_b, value_blk, preferred_element_type=j...]
    pallas_call x0 -> x1, Pallas kernels: none -> 46.2 us  [shards(): pl.pallas_call(functools.partial(kernel, seq_count, heads, group_size), o...]
    reduce_scatter x2 -> x0, waiting for transfers between devices: 23.6 us -> none  [the longest x1 23.2 us: shards(): lax.psum_scatter(key_sum, 'head', scatter_dimension=1, tiled=True)]
    ppermute x20 -> x0, waiting for transfers between devices: 19.6 us -> none  [from_behind(): lax.ppermute(value, axis, [(source, source + steps) for source in range(l...]
    all_gather x2 -> x0, blocking collectives: 11.1 us -> none  [the longest x1 5.66 us: shards(): lax.all_gather(trunk_values, 'head', axis=1, tiled=True)]
    reshape x8 -> x0, local copies, waits for them, and re-layouts: 9.65 us -> none  [the longest x4 4.84 us: grad_parts(): value_part.reshape(tok_rows, -1)]
    convert_element_type x7 -> x0, other arithmetic: 8.14 us -> none  [the longest x6 7.8 us: short(): return part.astype(jnp.bfloat16) if part.dtype == jnp.float32 else part]
  transfers between devices with their start and end apart: 22 -> 0, of which waited for: 10 -> 0; matrix products, arithmetic and copies ran while one was open for 32% -> 0% of each run, Pallas kernels for 0% -> 0%
where the time goes in v1:
time: 54.8 us; the launch traced here: 54.5 us
  Pallas kernels  46.2 us (84%)
  local copies, waits for them, and re-layouts  7.63 us (14%)
  between operations  0.65 us (1%)
    pallas_call x1, Pallas kernels, shards(): pl.pallas_call(functools.partial(kernel, seq_count, heads, group_size), o...  46.2 us
    unnamed x14, local copies, waits for them, and re-layouts  7.63 us

profile of v1, /device:TPU:0, one launch (start us, length us, event | category | flops | bytes accessed | tf_op | source)
XLA Modules:
  0.0 54.5 jit_solution(4174331118608993286)
XLA Ops:
  0.6 0.0 copy-start.4
  0.6 0.6 %copy-done.4 = s32[128]{0:T(128)S(1)} copy-done((s32[128]{0:T(128)S(1)}, s32[128]{0:T(128)}, u32[]{:S(2)}) %copy-start.4) | copy-done | bytes 536
  1.3 0.0 copy-start
  1.3 1.2 %copy-done = bf16[1,128,3584]{2,1,0:T(8,128)(2,1)S(1)} copy-done((bf16[1,128,3584]{2,1,0:T(8,128)(2,1)S(1)}, bf16[1,128,3584]{2,1,0:T(8,128)(2,1)}, u32[]{:S(2)}) %copy-start) | copy-done | bytes 917528
  2.5 0.0 copy-start.1
  2.5 1.2 %copy-done.1 = bf16[1,128,3584]{2,1,0:T(8,128)(2,1)S(1)} copy-done((bf16[1,128,3584]{2,1,0:T(8,128)(2,1)S(1)}, bf16[1,128,3584]{2,1,0:T(8,128)(2,1)}, u32[]{:S(2)}) %copy-start.1) | copy-done | bytes 917528
  3.6 0.0 copy-start.2
  3.6 0.8 %copy-done.2 = bf16[128,128]{1,0:T(8,128)(2,1)S(1)} copy-done((bf16[128,128]{1,0:T(8,128)(2,1)S(1)}, bf16[128,128]{1,0:T(8,128)(2,1)}, u32[]{:S(2)}) %copy-start.2) | copy-done | bytes 32792
  4.4 0.0 copy-start.3
  4.4 0.8 %copy-done.3 = bf16[128,128]{1,0:T(8,128)(2,1)S(1)} copy-done((bf16[128,128]{1,0:T(8,128)(2,1)S(1)}, bf16[128,128]{1,0:T(8,128)(2,1)}, u32[]{:S(2)}) %copy-start.3) | copy-done | bytes 32792
  5.2 46.2 %shard_map.84 = (bf16[1,128,3584]{2,1,0:T(8,128)(2,1)S(1)}, bf16[1,128,3584]{2,1,0:T(8,128)(2,1)S(1)}, f32[128,128]{1,0:T(8,128)S(1)}, f32[128,128]{1,0:T(8,128)S(1)}) custom-call(bf16[1,128,3584]{2,1,0:T(8,128)(2,1)S(1)} %copy-done, bf16[128,128]{1,0:T(8,128)(2,1)S(1)} %copy-done.2, bf16[128,128]{1,0:T(8,128)(2,1)S(1)} %copy-done.3, ...), custom_call_target="tpu_custom_call" | custom-call | flops 3523215360 | bytes 3670016 | tf_op jit(solution)/shard_map/pallas_call | solution.py:284
  51.4 0.9 %copy.13 = bf16[1,128,3584]{2,1,0:T(8,128)(2,1)} copy(bf16[1,128,3584]{2,1,0:T(8,128)(2,1)S(1)} %get-tuple-element.8) | data formatting | bytes 1835008
  52.3 0.9 %copy.14 = bf16[1,128,3584]{2,1,0:T(8,128)(2,1)} copy(bf16[1,128,3584]{2,1,0:T(8,128)(2,1)S(1)} %get-tuple-element.9) | data formatting | bytes 1835008
  53.2 0.6 %copy.15 = f32[128,128]{1,0:T(8,128)} copy(f32[128,128]{1,0:T(8,128)S(1)} %get-tuple-element.10) | data formatting | bytes 131072
  53.9 0.6 %copy.16 = f32[128,128]{1,0:T(8,128)} copy(f32[128,128]{1,0:T(8,128)S(1)} %get-tuple-element.11) | data formatting | bytes 131072
Async XLA Ops:
  0.6 0.7 %copy-start.4 = (s32[128]{0:T(128)S(1)}, s32[128]{0:T(128)}, u32[]{:S(2)}) copy-start(s32[128]{0:T(128)} %param.9) | copy-start | bytes 1540
  1.3 1.2 %copy-start = (bf16[1,128,3584]{2,1,0:T(8,128)(2,1)S(1)}, bf16[1,128,3584]{2,1,0:T(8,128)(2,1)}, u32[]{:S(2)}) copy-start(bf16[1,128,3584]{2,1,0:T(8,128)(2,1)} %q_hbm.1) | copy-start | bytes 2752516
  2.5 1.2 %copy-start.1 = (bf16[1,128,3584]{2,1,0:T(8,128)(2,1)S(1)}, bf16[1,128,3584]{2,1,0:T(8,128)(2,1)}, u32[]{:S(2)}) copy-start(bf16[1,128,3584]{2,1,0:T(8,128)(2,1)} %g_hbm.1) | copy-start | bytes 2752516
  3.6 0.8 %copy-start.2 = (bf16[128,128]{1,0:T(8,128)(2,1)S(1)}, bf16[128,128]{1,0:T(8,128)(2,1)}, u32[]{:S(2)}) copy-start(bf16[128,128]{1,0:T(8,128)(2,1)} %k_ref.1) | copy-start | bytes 98308
  4.4 0.8 %copy-start.3 = (bf16[128,128]{1,0:T(8,128)(2,1)S(1)}, bf16[128,128]{1,0:T(8,128)(2,1)}, u32[]{:S(2)}) copy-start(bf16[128,128]{1,0:T(8,128)(2,1)} %v_ref.1) | copy-start | bytes 98308

commit v2 on v1

--- a/solution.py
+++ b/solution.py
@@ -156,28 +156,30 @@
             kc[at * rows:(at + 1) * rows, :] = kv[slot, hop, 0:rows, :]
             vc[at * rows:(at + 1) * rows, :] = kv[slot, hop, rows:2 * rows, :]
 
-        for r in range(group_size):
-            cols = slice(r * DH, (r + 1) * DH)
-            q = qbuf[slot, :, cols]
-            g = gbuf[slot, :, cols]
-            t = fold(dot(q, kc[...], NT)) * (scaling * math.log2(math.e)) + bias[...]
-            e = jnp.exp2(t - jnp.max(t, axis=1, keepdims=True))
-            probs = e * (1.0 / jnp.sum(e, axis=1, keepdims=True))
-            probs_b = unfold(probs)
-            pscr[r * rows:(r + 1) * rows, :] = probs_b
-            out32 = dot(probs_b, vc[...], NN)
-            obuf[slot, :, cols] = out32.astype(jnp.bfloat16)
-            delta = jnp.sum(g.astype(jnp.float32) * out32, axis=1, keepdims=True)
-            dprobs = fold(dot(g, vc[...], NT))
-            dscores_b = unfold(probs * (dprobs - delta))
-            dscr[r * rows:(r + 1) * rows, :] = dscores_b
-            dqbuf[slot, :, cols] = (dot(dscores_b, kc[...], NN) * scaling).astype(jnp.bfloat16)
-        store(slot, 0).start()
-        store(slot, 1).start()
         q_rows = jnp.concatenate(
             [qbuf[slot, :, r * DH:(r + 1) * DH] for r in range(group_size)], axis=0)
         g_rows = jnp.concatenate(
             [gbuf[slot, :, r * DH:(r + 1) * DH] for r in range(group_size)], axis=0)
+        raw = dot(q_rows, kc[...], NT)
+        dprobs = dot(g_rows, vc[...], NT)
+        for r in range(group_size):
+            here = slice(r * rows, (r + 1) * rows)
+            t = fold(raw[here]) * (scaling * math.log2(math.e)) + bias[...]
+            e = jnp.exp2(t - jnp.max(t, axis=1, keepdims=True))
+            probs = e * (1.0 / jnp.sum(e, axis=1, keepdims=True))
+            pscr[here, :] = unfold(probs)
+            weighted = probs * fold(dprobs[here])
+            delta = jnp.sum(weighted, axis=1, keepdims=True)
+            dscr[here, :] = unfold(weighted - probs * delta)
+        out32 = dot(pscr[...], vc[...], NN)
+        dq32 = dot(dscr[...], kc[...], NN) * scaling
+        for r in range(group_size):
+            here = slice(r * rows, (r + 1) * rows)
+            cols = slice(r * DH, (r + 1) * DH)
+            obuf[slot, :, cols] = out32[here].astype(jnp.bfloat16)
+            dqbuf[slot, :, cols] = dq32[here].astype(jnp.bfloat16)
+        store(slot, 0).start()
+        store(slot, 1).start()
         key_t = dot(q_rows, dscr[...], TN) * scaling
         value_t = dot(g_rows, pscr[...], TN)
         for at, hop in enumerate(BLOCK_ORDER):
@@ -307,7 +309,7 @@
             dma((3,)), dma((3,)), dma((SPAN,)), dma((SPAN,)),
         ],
         compiler_params=pltpu.CompilerParams(
-            collective_id=0, has_side_effects=True, vmem_limit_bytes=40 * 1024 * 1024),
+            collective_id=0, has_side_effects=True, vmem_limit_bytes=62 * 1024 * 1024),
         cost_estimate=pl.CostEstimate(
             flops=12 * rows * rows * HOPS * width, bytes_accessed=8 * rows * width,
             transcendentals=rows * rows * HOPS * width // DH),

time: 54.8 us -> 44.9 us (0.82)
  Pallas kernels: 46.2 us -> 39.3 us
  local copies, waits for them, and re-layouts: 7.63 us -> 4.66 us
    pallas_call x1, Pallas kernels: 46.2 us -> 39.3 us  [shards(): pl.pallas_call(functools.partial(kernel, seq_count, heads, group_size), o...]
    unnamed x14 -> x10, local copies, waits for them, and re-layouts: 7.63 us -> 4.66 us
where the time goes in v2:
time: 44.9 us; the launch traced here: 44.6 us
  Pallas kernels  39.3 us (88%)
  local copies, waits for them, and re-layouts  4.66 us (10%)
  between operations  0.65 us (1%)
    pallas_call x1, Pallas kernels, shards(): pl.pallas_call(functools.partial(kernel, seq_count, heads, group_size), o...  39.3 us
    unnamed x10, local copies, waits for them, and re-layouts  4.66 us

profile of v2, /device:TPU:0, one launch (start us, length us, event | category | flops | bytes accessed | tf_op | source)
XLA Modules:
  0.0 44.6 jit_solution(2626176504306827819)
XLA Ops:
  0.6 39.3 %shard_map.84 = (bf16[1,128,3584]{2,1,0:T(8,128)(2,1)}, bf16[1,128,3584]{2,1,0:T(8,128)(2,1)}, f32[128,128]{1,0:T(8,128)}, f32[128,128]{1,0:T(8,128)}) custom-call(bf16[1,128,3584]{2,1,0:T(8,128)(2,1)} %q_hbm.1, bf16[128,128]{1,0:T(8,128)(2,1)} %k_ref.1, bf16[128,128]{1,0:T(8,128)(2,1)} %v_ref.1, bf16[1,128,3584]{2,1,0:T(8,128)(2,1)} %g_hbm.1, s32[1,128]{1,0:T(1,128)} %bitcast.1), custom_call_target="tpu_custom_call" | custom-call | flops 3523215360 | bytes 3670016 | tf_op jit(solution)/shard_map/pallas_call | solution.py:286
  39.9 0.0 copy-start
  40.0 2.2 %copy.13 = bf16[1,128,3584]{2,1,0:T(8,128)(2,1)} copy(bf16[1,128,3584]{2,1,0:T(8,128)(2,1)} %get-tuple-element.8) | data formatting | bytes 1835008
  42.2 0.0 copy-done
  42.2 0.0 copy-start.2
  42.2 0.9 %copy.14 = bf16[1,128,3584]{2,1,0:T(8,128)(2,1)} copy(bf16[1,128,3584]{2,1,0:T(8,128)(2,1)S(1)} %copy-done) | data formatting | bytes 1835008
  43.1 0.0 copy-done.2
  43.1 0.0 copy-start.1
  43.1 0.6 %copy.15 = f32[128,128]{1,0:T(8,128)} copy(f32[128,128]{1,0:T(8,128)S(1)} %copy-done.2) | data formatting | bytes 131072
  43.8 0.2 copy-done.1
  44.0 0.6 %copy.16 = f32[128,128]{1,0:T(8,128)} copy(f32[128,128]{1,0:T(8,128)S(1)} %copy-done.1) | data formatting | bytes 131072
Async XLA Ops:
  39.9 2.3 %copy-start = (bf16[1,128,3584]{2,1,0:T(8,128)(2,1)S(1)}, bf16[1,128,3584]{2,1,0:T(8,128)(2,1)}, u32[]{:S(2)}) copy-start(bf16[1,128,3584]{2,1,0:T(8,128)(2,1)} %get-tuple-element.9) | copy-start | bytes 2752516
  42.2 0.9 %copy-start.2 = (f32[128,128]{1,0:T(8,128)S(1)}, f32[128,128]{1,0:T(8,128)}, u32[]{:S(2)}) copy-start(f32[128,128]{1,0:T(8,128)} %get-tuple-element.10) | copy-start | bytes 196612
  43.1 0.9 %copy-start.1 = (f32[128,128]{1,0:T(8,128)S(1)}, f32[128,128]{1,0:T(8,128)}, u32[]{:S(2)}) copy-start(f32[128,128]{1,0:T(8,128)} %get-tuple-element.11) | copy-start | bytes 196612

commit v3 on v2

--- a/solution.py
+++ b/solution.py
@@ -12,6 +12,8 @@
 SPAN = 4
 HOPS = SPAN + 1
 BLOCK_ORDER = (1, 2, 3, 0, 4)
+PARTS = ((3, 2), (1, 2), (0, 1))
+PIECES = 1
 MESH = pl.DeviceIdType.MESH
 NT = (((1,), (1,)), ((), ()))
 NN = (((1,), (0,)), ((), ()))
@@ -24,16 +26,16 @@
 
 def kernel(
     seq_count, heads, group_size,
-    q_hbm, k_ref, v_ref, g_hbm, seg_ref,
+    q_hbm, k_hbm, v_hbm, g_hbm, seg_hbm,
     out_hbm, dq_hbm, dk_ref, dv_ref,
-    kv, qbuf, gbuf, obuf, dqbuf, kc, vc, bias, pscr, dscr,
+    seg, kv, qbuf, gbuf, obuf, dqbuf, kc, vc, bias, pscr, dscr,
     grad_own, grad_send, grad_recv, seq_send, seq_recv,
-    in_sem, out_sem, kv_recv, kv_seq_send, kv_head_send,
+    own_sem, in_sem, out_sem, kv_recv, kv_seq_send, kv_head_send,
     gr_send, gr_recv, sq_send, sq_recv,
 ):
     m = lax.axis_index("head")
     s = lax.axis_index("seq")
-    rows = k_ref.shape[0]
+    rows = k_hbm.shape[0]
     slab = group_size * DH
     scaling = 1.0 / math.sqrt(DH)
     core_peer = m + 1 - 2 * (m % 2)
@@ -71,14 +73,13 @@
     def kv_arrived(slot, hop):
         kv_head(slot, hop).wait_recv()
 
-    for slot in (0, 1, 2, 3):
-        load(slot, 0).start()
-        load(slot, 1).start()
-
-    kv[0, 0, 0:rows, :] = k_ref[...]
-    kv[0, 0, rows:2 * rows, :] = v_ref[...]
-    kv[0, 0, 2 * rows:, :] = jnp.broadcast_to(
-        seg_ref[...].astype(jnp.float32), (16, rows)).astype(jnp.bfloat16)
+    own = (
+        pltpu.make_async_copy(k_hbm, kv.at[0, 0, 0:rows, :], own_sem.at[0]),
+        pltpu.make_async_copy(v_hbm, kv.at[0, 0, rows:2 * rows, :], own_sem.at[1]),
+        pltpu.make_async_copy(seg_hbm, seg, own_sem.at[2]),
+    )
+    for copy in own:
+        copy.start()
 
     barrier = pltpu.get_barrier_semaphore()
     for peer in (core_peer, x_peer):
@@ -91,6 +92,14 @@
         def _(step=step):
             pl.semaphore_signal(barrier, inc=1, device_id=(m, s + step), device_id_type=MESH)
         expected = expected + jnp.where(valid, 1, 0)
+
+    for copy in own:
+        copy.wait()
+    for slot in (0, 1, 2, 3):
+        load(slot, 0).start()
+        load(slot, 1).start()
+    kv[0, 0, 2 * rows:, :] = jnp.broadcast_to(
+        seg[...].astype(jnp.float32), (16, rows)).astype(jnp.bfloat16)
     pl.semaphore_wait(barrier, expected)
 
     for hop in (1, 2):
@@ -191,29 +200,37 @@
                 grad_send[slot - 1, hop, 0:DH, :] = key_t[:, cols].astype(jnp.bfloat16)
                 grad_send[slot - 1, hop, DH:, :] = value_t[:, cols].astype(jnp.bfloat16)
 
-    def gr_copy(slot):
-        return remote(grad_send.at[slot - 1], grad_recv.at[slot - 1], gr_send.at[slot - 1],
-                      gr_recv.at[slot - 1], x_peer if slot == 2 else core_peer, s)
+    def gr_copy(slot, part):
+        hops = pl.ds(*PARTS[part])
+        return remote(grad_send.at[slot - 1, hops], grad_recv.at[slot - 1, hops],
+                      gr_send.at[slot - 1, part], gr_recv.at[slot - 1, part],
+                      x_peer if slot == 2 else core_peer, s)
 
     compute(0)
     for hop in (2, 3, 4):
         kv_arrived(2, hop)
         kv_head(3, hop).start()
     for hop in range(HOPS):
+        kv_arrived(1, hop)
+    compute(1)
+    for part in range(len(PARTS)):
+        gr_copy(1, part).start()
+    compute(2)
+    for hop in range(HOPS):
         kv_arrived(3, hop)
     compute(3)
-    gr_copy(3).start()
-    compute(2)
-    gr_copy(3).wait_recv()
-    grad_send[1] = (grad_send[1].astype(jnp.float32)
-                    + grad_recv[2].astype(jnp.float32)).astype(jnp.bfloat16)
-    gr_copy(2).start()
-    for hop in range(HOPS):
-        kv_arrived(1, hop)
-    compute(1)
-    gr_copy(1).start()
-    gr_copy(1).wait_recv()
-    gr_copy(2).wait_recv()
+    for part in range(len(PARTS)):
+        gr_copy(3, part).start()
+    for part, (first, count) in enumerate(PARTS):
+        hops = slice(first, first + count)
+        gr_copy(3, part).wait_recv()
+        grad_send[1, hops] = (grad_send[1, hops].astype(jnp.float32)
+                              + grad_recv[2, hops].astype(jnp.float32)).astype(jnp.bfloat16)
+        gr_copy(2, part).start()
+
+    def gr_arrived(part):
+        gr_copy(1, part).wait_recv()
+        gr_copy(2, part).wait_recv()
 
     def total(hop):
         return (grad_own[hop] + grad_recv[0, hop].astype(jnp.float32)
@@ -223,11 +240,13 @@
         return remote(seq_send.at[hop - 1], seq_recv.at[hop - 1], sq_send.at[hop - 1],
                       sq_recv.at[hop - 1], m, s - (hop if hop <= 2 else 2))
 
+    gr_arrived(0)
     for hop in (4, 3):
         @pl.when(s >= hop)
         def _(hop=hop):
             seq_send[hop - 1] = total(hop).astype(jnp.bfloat16)
             sq_copy(hop).start()
+    gr_arrived(1)
     for hop in (2, 1):
         grad_own[hop] = total(hop)
 
@@ -240,6 +259,7 @@
         def _(hop=hop):
             seq_send[hop - 1] = grad_own[hop].astype(jnp.bfloat16)
             sq_copy(hop).start()
+    gr_arrived(2)
     grad_own[0] = total(0)
     for hop in (2, 1):
         @pl.when(s < seq_count - hop)
@@ -263,11 +283,32 @@
     for slot in (1, 2, 3):
         for hop in range(HOPS):
             kv_head(slot, hop).wait_send()
-        gr_copy(slot).wait_send()
+        for part in range(len(PARTS)):
+            gr_copy(slot, part).wait_send()
     for hop in range(1, HOPS):
         @pl.when(s >= hop)
         def _(hop=hop):
             sq_copy(hop).wait_send()
+
+
+def hand_over(a, b, c, d, a_out, b_out, c_out, d_out, a_on, b_on, c_on, d_on, in_sem, out_sem):
+    loads, stores = [], []
+    for at, (src, on, dst) in enumerate(
+            ((a, a_on, a_out), (b, b_on, b_out), (c, c_on, c_out), (d, d_on, d_out))):
+        pieces = PIECES if len(src.shape) == 3 else 1
+        size = src.shape[-2] // pieces
+        for n in range(pieces):
+            part = pl.ds(n * size, size)
+            part = (0, part) if len(src.shape) == 3 else (part,)
+            loads.append(pltpu.make_async_copy(src.at[part], on.at[part], in_sem.at[at, n]))
+            stores.append(pltpu.make_async_copy(on.at[part], dst.at[part], out_sem.at[at, n]))
+    for load in loads:
+        load.start()
+    for load, store in zip(loads, stores):
+        load.wait()
+        store.start()
+    for store in stores:
+        store.wait()
 
 
 def shards(queries, trunk_keys, trunk_values, out_grad, segment_ids):
@@ -278,17 +319,19 @@
     group_size = width // (DH * heads)
     slab = group_size * DH
     vmem = pl.BlockSpec(memory_space=pltpu.VMEM)
-    hbm = pl.BlockSpec(memory_space=pl.ANY)
+    hbm = pl.BlockSpec(memory_space=pltpu.HBM)
+    free = pl.BlockSpec(memory_space=pl.ANY)
     bf16, f32 = jnp.bfloat16, jnp.float32
     dma = pltpu.SemaphoreType.DMA
     big = jax.ShapeDtypeStruct(queries.shape, bf16)
     small = jax.ShapeDtypeStruct(trunk_keys.shape, f32)
-    return tuple(pl.pallas_call(
+    results = pl.pallas_call(
         functools.partial(kernel, seq_count, heads, group_size),
         out_shape=(big, big, small, small),
-        in_specs=[hbm, vmem, vmem, hbm, vmem],
-        out_specs=(hbm, hbm, vmem, vmem),
+        in_specs=[hbm] * 5,
+        out_specs=(free, free, vmem, vmem),
         scratch_shapes=[
+            pltpu.VMEM((1, rows), jnp.int32),
             pltpu.VMEM((heads, HOPS, 2 * rows + 16, DH), bf16),
             pltpu.VMEM((heads, rows, slab), bf16),
             pltpu.VMEM((heads, rows, slab), bf16),
@@ -304,16 +347,28 @@
             pltpu.VMEM((3, HOPS, 2 * DH, rows), bf16),
             pltpu.VMEM((SPAN, 2 * DH, rows), bf16),
             pltpu.VMEM((SPAN, 2 * DH, rows), bf16),
-            dma((2, heads)), dma((2, heads)),
+            dma((3,)), dma((2, heads)), dma((2, heads)),
             dma((heads, HOPS)), dma((HOPS,)), dma((heads, HOPS)),
-            dma((3,)), dma((3,)), dma((SPAN,)), dma((SPAN,)),
+            dma((3, len(PARTS))), dma((3, len(PARTS))), dma((SPAN,)), dma((SPAN,)),
         ],
         compiler_params=pltpu.CompilerParams(
             collective_id=0, has_side_effects=True, vmem_limit_bytes=62 * 1024 * 1024),
         cost_estimate=pl.CostEstimate(
             flops=12 * rows * rows * HOPS * width, bytes_accessed=8 * rows * width,
             transcendentals=rows * rows * HOPS * width // DH),
-    )(queries, trunk_keys, trunk_values, out_grad, segment_ids.reshape(1, rows)))
+    )(queries, trunk_keys, trunk_values, out_grad, segment_ids.reshape(1, rows))
+    return tuple(pl.pallas_call(
+        hand_over,
+        out_shape=(big, big, small, small),
+        in_specs=[free] * 4,
+        out_specs=(free,) * 4,
+        scratch_shapes=[
+            pltpu.VMEM(big.shape, bf16), pltpu.VMEM(big.shape, bf16),
+            pltpu.VMEM(small.shape, f32), pltpu.VMEM(small.shape, f32),
+            dma((4, PIECES)), dma((4, PIECES)),
+        ],
+        compiler_params=pltpu.CompilerParams(vmem_limit_bytes=62 * 1024 * 1024),
+    )(*results))
 
 
 def solution(mesh):

time: 44.9 us -> 40 us (0.89)
  the two profiles are of different devices: /device:TPU:0 before, /device:TPU:13 now
where the time goes in v3:
time: 40 us; the launch traced here: 39.8 us
  Pallas kernels  39.2 us (98%)
  between operations  0.64 us (2%)
    pallas_call x1, Pallas kernels, shards(): pl.pallas_call(functools.partial(kernel, seq_count, heads, group_size), o...  36.6 us
    pallas_call x1, Pallas kernels, shards(): pl.pallas_call(hand_over, out_shape=(big, big, small, small), in_specs=[f...  2.5 us

profile of v3, /device:TPU:13, one launch (start us, length us, event | category | flops | bytes accessed | tf_op | source)
XLA Modules:
  0.0 39.8 jit_solution(567985469623616089)
XLA Ops:
  0.6 36.6 %shard_map.84 = (bf16[1,128,3584]{2,1,0:T(8,128)(2,1)}, bf16[1,128,3584]{2,1,0:T(8,128)(2,1)}, f32[128,128]{1,0:T(8,128)}, f32[128,128]{1,0:T(8,128)}) custom-call(bf16[1,128,3584]{2,1,0:T(8,128)(2,1)} %q_hbm.1, bf16[128,128]{1,0:T(8,128)(2,1)} %k_hbm.1, bf16[128,128]{1,0:T(8,128)(2,1)} %v_hbm.1, bf16[1,128,3584]{2,1,0:T(8,128)(2,1)} %g_hbm.1, s32[1,128]{1,0:T(1,128)} %bitcast.1), custom_call_target="tpu_custom_call" | custom-call | flops 3523215360 | bytes 3670016 | tf_op jit(solution)/shard_map/pallas_call | solution.py:328
  37.3 2.5 %shard_map.85 = (bf16[1,128,3584]{2,1,0:T(8,128)(2,1)}, bf16[1,128,3584]{2,1,0:T(8,128)(2,1)}, f32[128,128]{1,0:T(8,128)}, f32[128,128]{1,0:T(8,128)}) custom-call(bf16[1,128,3584]{2,1,0:T(8,128)(2,1)} %get-tuple-element.8.a, bf16[1,128,3584]{2,1,0:T(8,128)(2,1)} %get-tuple-element.9.b, f32[128,128]{1,0:T(8,128)} %get-tuple-element.10.c, ...), custom_call_target="tpu_custom_call" | custom-call | tf_op jit(solution)/shard_map/pallas_call | solution.py:360

commit v4 on v3

--- a/solution.py
+++ b/solution.py
@@ -12,7 +12,8 @@
 SPAN = 4
 HOPS = SPAN + 1
 BLOCK_ORDER = (1, 2, 3, 0, 4)
-PARTS = ((3, 2), (1, 2), (0, 1))
+PART_HOPS = (4, 3, 2, 1, 0)
+PARTS = tuple((hop, 1) for hop in PART_HOPS)
 PIECES = 1
 MESH = pl.DeviceIdType.MESH
 NT = (((1,), (1,)), ((), ()))
@@ -240,14 +241,15 @@
         return remote(seq_send.at[hop - 1], seq_recv.at[hop - 1], sq_send.at[hop - 1],
                       sq_recv.at[hop - 1], m, s - (hop if hop <= 2 else 2))
 
-    gr_arrived(0)
-    for hop in (4, 3):
+    for hop in PART_HOPS[:2]:
+        gr_arrived(PART_HOPS.index(hop))
+
         @pl.when(s >= hop)
         def _(hop=hop):
             seq_send[hop - 1] = total(hop).astype(jnp.bfloat16)
             sq_copy(hop).start()
-    gr_arrived(1)
-    for hop in (2, 1):
+    for hop in PART_HOPS[2:4]:
+        gr_arrived(PART_HOPS.index(hop))
         grad_own[hop] = total(hop)
 
         @pl.when((s >= hop) & (s < seq_count - 2))
@@ -259,7 +261,7 @@
         def _(hop=hop):
             seq_send[hop - 1] = grad_own[hop].astype(jnp.bfloat16)
             sq_copy(hop).start()
-    gr_arrived(2)
+    gr_arrived(4)
     grad_own[0] = total(0)
     for hop in (2, 1):
         @pl.when(s < seq_count - hop)

time: 40 us -> 39 us (0.975)
  the two profiles are of different devices: /device:TPU:13 before, /device:TPU:0 now
where the time goes in v4:
time: 39 us; the launch traced here: 38.8 us
  Pallas kernels  38.1 us (98%)
  between operations  0.64 us (2%)
    pallas_call x1, Pallas kernels, shards(): pl.pallas_call(functools.partial(kernel, seq_count, heads, group_size), o...  35.6 us
    pallas_call x1, Pallas kernels, shards(): pl.pallas_call(hand_over, out_shape=(big, big, small, small), in_specs=[f...  2.5 us

profile of v4, /device:TPU:0, one launch (start us, length us, event | category | flops | bytes accessed | tf_op | source)
XLA Modules:
  0.0 38.8 jit_solution(982309636370381976)
XLA Ops:
  0.6 35.6 %shard_map.84 = (bf16[1,128,3584]{2,1,0:T(8,128)(2,1)}, bf16[1,128,3584]{2,1,0:T(8,128)(2,1)}, f32[128,128]{1,0:T(8,128)}, f32[128,128]{1,0:T(8,128)}) custom-call(bf16[1,128,3584]{2,1,0:T(8,128)(2,1)} %q_hbm.1, bf16[128,128]{1,0:T(8,128)(2,1)} %k_hbm.1, bf16[128,128]{1,0:T(8,128)(2,1)} %v_hbm.1, bf16[1,128,3584]{2,1,0:T(8,128)(2,1)} %g_hbm.1, s32[1,128]{1,0:T(1,128)} %bitcast.1), custom_call_target="tpu_custom_call" | custom-call | flops 3523215360 | bytes 3670016 | tf_op jit(solution)/shard_map/pallas_call | solution.py:330
  36.2 2.5 %shard_map.85 = (bf16[1,128,3584]{2,1,0:T(8,128)(2,1)}, bf16[1,128,3584]{2,1,0:T(8,128)(2,1)}, f32[128,128]{1,0:T(8,128)}, f32[128,128]{1,0:T(8,128)}) custom-call(bf16[1,128,3584]{2,1,0:T(8,128)(2,1)} %get-tuple-element.8.a, bf16[1,128,3584]{2,1,0:T(8,128)(2,1)} %get-tuple-element.9.b, f32[128,128]{1,0:T(8,128)} %get-tuple-element.10.c, ...), custom_call_target="tpu_custom_call" | custom-call | tf_op jit(solution)/shard_map/pallas_call | solution.py:362
